TPU v7x, 32 devices: a whole 2x2x4 slice. The times are simulated.
32 devices in a mesh: groups: 2 (over y), row: 8 (over z, x), col: 2 (over core).
Axes of the slice: x: 2, y: 2, z: 4, core: 2. Of those that a mesh axis runs over, the one named last changes fastest.
Arguments:
- tokens: bfloat16 [512, 8192], P(('groups', 'col'), 'row'), parts along dimension 0, may hold values from -6 to 6
- gate_weight: bfloat16 [16384, 26624], P(('groups', 'row'), 'col'), parts along dimension 0, may hold values from -6 to 6
- up_weight: bfloat16 [8192, 26624], P('row', 'col'), may hold values from -6 to 6
- gate_up_left: bfloat16 [4, 8192, 128], P(None, 'row'), may hold values from -6 to 6
- gate_up_right: bfloat16 [4, 2, 64, 26624], P(None, None, None, ('col', 'row')), may hold values from -0.3984375 to 0.3984375
- adapter_ids: int32 [4], P('groups'), parts along dimension 0, may hold values from 0 to 3
Outputs:
- gate_merged: bfloat16 [16384, 26624], P(('groups', 'row'), 'col'), parts along dimension 0
- hidden: bfloat16 [512, 26624], P('groups', ('col', 'row')), parts along dimension 0
There are 2 independent parts, one for each index of `groups`. A program takes and returns all parts, laid end to end along the dimension named above; an argument that names none is the same for every part. Nothing has to cross between parts.
All inputs are finite; a program needn't handle non-finite values.
Results may differ from a plain program's by a relative error of at most 0.005.
Values may be sent and summed in bfloat16 or wider, within the bound.
A program may use at most 256 MiB of HBM per device.

v0:
```python
import jax
import jax.numpy as jnp
from jax import lax
from jax.sharding import PartitionSpec as P


def merge_panel(weight, left_panel, right_panel):
    update = jnp.dot(left_panel, right_panel, preferred_element_type=jnp.float32)
    return (weight.astype(jnp.float32) + update).astype(jnp.bfloat16)


def per_device(tokens, gate_weight, up_weight, gate_up_left, gate_up_right, adapter_ids):
    adapter_rank_size = gate_up_right.shape[2]
    old_id = adapter_ids[0]
    new_id = adapter_ids[1]
    incoming_left = gate_up_left[new_id]
    outgoing_left = gate_up_left[old_id]
    gate_left_panel = jnp.concatenate(
        [incoming_left[:, :adapter_rank_size], -outgoing_left[:, :adapter_rank_size]], axis=1
    )
    right_chosen = jnp.concatenate([gate_up_right[new_id, 0], gate_up_right[old_id, 0]], axis=0)
    right_all = lax.all_gather(right_chosen, "row", axis=1, tiled=True)
    gate_merged = merge_panel(gate_weight, gate_left_panel, right_all)
    entire_result = lax.all_gather(tokens, "col", axis=0, tiled=True)
    full_width = entire_result.shape[1] * lax.axis_size("row")
    scale_factor = float(full_width) ** (-0.5)
    low_rank_part = jnp.dot(
        entire_result, incoming_left[:, adapter_rank_size:], preferred_element_type=jnp.float32
    )
    low_rank_term = (lax.psum(low_rank_part, "row") * scale_factor).astype(jnp.bfloat16)
    token_count = entire_result.shape[0]
    contract = (((0,), (1,)), ((), ()))
    gate_term = lax.dot_general(
        gate_merged, entire_result, contract, preferred_element_type=jnp.float32
    )
    up_term = lax.dot_general(
        up_weight, entire_result, contract, preferred_element_type=jnp.float32
    )
    summed = lax.psum_scatter(
        jnp.concatenate([gate_term, up_term], axis=1), "row", scatter_dimension=0, tiled=True
    )
    gate_value = summed[:, :token_count].T * scale_factor
    up_base = summed[:, token_count:].T * scale_factor
    up_value = up_base + jnp.dot(
        low_rank_term, gate_up_right[new_id, 1], preferred_element_type=jnp.float32
    )
    hidden = (jax.nn.silu(gate_value) * up_value).astype(jnp.bfloat16)
    return (gate_merged, hidden)


def solution(mesh):
    return jax.shard_map(
        per_device,
        mesh=mesh,
        in_specs=(
            P(("groups", "col"), "row"),
            P(("groups", "row"), "col"),
            P("row", "col"),
            P(None, "row", None),
            P(None, None, None, ("col", "row")),
            P("groups"),
        ),
        out_specs=(P(("groups", "row"), "col"), P("groups", ("col", "row"))),
        check_vma=False,
    )
```

profile of v0, /device:TPU:0, one launch (start us, length us, event | category | flops | bytes accessed | tf_op | source)
XLA Modules:
  0.0 598.9 jit_solution(7489299865126817959)
XLA Ops:
  7.2 0.0 all-gather.2.cloned.1.call-start
  7.2 1.3 fusion.15
  12.4 1.1 dynamic-slice_bitcast_fusion.3
  13.5 0.8 pad_maximum_fusion.1
  14.3 0.0 all-gather.2.cloned.1.call-update
  14.3 0.0 all-reduce.2.cloned.1.call-start
  14.3 1.1 dynamic-slice_bitcast_fusion.1
  15.4 2.5 all_gather.7
  17.9 1.0 convolution_bitcast_fusion
  18.9 0.0 all-reduce.2.cloned.1.call-update
  18.9 0.0 reduce-scatter.2.cloned.1.call-start
  19.0 19.4 %fusion.17 = f32[13312,256]{0,1:T(8,128)} fusion(bf16[256,1024]{1,0:T(8,128)(2,1)S(1)} %all_gather.7, bf16[1024,13312]{1,0:T(8,128)(2,1)} %param.8), kind=kOutput, calls=%fused_computation.30 | convolution fusion | flops 6979321856 | bytes 41418752 | tf_op jit(solution)/shard_map/dot_general | solution.py:36
  38.4 42.2 %all-gather.2.cloned.1.call-done = bf16[128,13312]{1,0:T(8,128)(2,1)} async-done(((bf16[128,1664]{1,0:T(8,128)(2,1)}), bf16[128,13312]{1,0:T(8,128)(2,1)}) %all-gather.2.cloned.1.call-update) | async-done | bytes 3407888 | tf_op jit(solution)/shard_map/all_gather | solution.py:22
  80.6 23.1 %add_convert_fusion = bf16[1024,13312]{1,0:T(8,128)(2,1)} fusion(bf16[1024,13312]{1,0:T(8,128)(2,1)} %param.7, bf16[128,13312]{1,0:T(8,128)(2,1)} %all-gather.2.cloned.1.call-done, bf16[1024,64]{1,0:T(8,128)(2,1)S(1)} %slice_negate_fusion, bf16[1024,64]{1,0:T(8,128)(2,1)S(1)} %bitcast.30), kind=kOutput, calls=%fused_computation | convolution fusion | flops 3531079680 | bytes 58195968 | tf_op jit(solution)/shard_map/dot_general | solution.py:8
  103.7 19.1 %fusion.16 = f32[13312,256]{0,1:T(8,128)} fusion(bf16[256,1024]{1,0:T(8,128)(2,1)S(1)} %all_gather.7, bf16[1024,13312]{1,0:T(8,128)(2,1)} %add_convert_fusion), kind=kOutput, calls=%fused_computation.29 | convolution fusion | flops 6979321856 | bytes 41418752 | tf_op jit(solution)/shard_map/dot_general | solution.py:33
  122.8 20.3 %pad_maximum_fusion = f32[13312,512]{0,1:T(8,128)} fusion(f32[13312,256]{0,1:T(8,128)} %fusion.17, f32[13312,256]{0,1:T(8,128)} %fusion.16), kind=kLoop, calls=%fused_computation.1 | loop fusion | flops 6815744 | bytes 54525952 | tf_op jit(solution)/shard_map/concatenate | solution.py:40
  143.1 0.0 reduce-scatter.2.cloned.1.call-update
  143.1 8.0 %all-reduce.2.cloned.1.call-done = f32[256,64]{0,1:T(8,128)} async-done(((f32[256,64]{0,1:T(8,128)}), f32[256,64]{0,1:T(8,128)}) %all-reduce.2.cloned.1.call-update) | async-done | bytes 65552 | tf_op jit(solution)/shard_map/psum | solution.py:30
  151.1 437.5 %reduce-scatter.2.cloned.1.call-done = f32[1664,512]{0,1:T(8,128)} async-done(((f32[13312,512]{0,1:T(8,128)}), f32[1664,512]{0,1:T(8,128)}) %reduce-scatter.2.cloned.1.call-update) | async-done | bytes 3407888 | tf_op jit(solution)/shard_map/reduce_scatter | solution.py:39
  588.6 3.8 fusion.1
  (1 shorter events, 0.0 us)
Async XLA Ops:
  7.2 73.4 %all-gather.2.cloned.1.call-start = ((), (), s32[]{:S(2)}) async-start(), calls=%async_computation.1 | async-start | bytes 3833856 | tf_op jit(solution)/shard_map/all_gather | solution.py:22
  14.3 136.8 %all-reduce.2.cloned.1.call-start = ((), (), s32[]{:S(2)}) async-start(), calls=%async_computation.3 | async-start | bytes 131072 | tf_op jit(solution)/shard_map/psum | solution.py:30
  18.9 569.7 %reduce-scatter.2.cloned.1.call-start = ((), (), s32[]{:S(2)}) async-start(), calls=%async_computation.2 | async-start | bytes 30670848 | tf_op jit(solution)/shard_map/reduce_scatter | solution.py:39
Sparse Core Ops, SparseCore 0:
  14.4 66.1 all-gather.1
  84.0 67.0 all-reduce.1
  155.0 433.5 reduce-scatter.1
where the time goes:
time: 599 us
  waiting for transfers between devices  488 us (81%)
  matrix products  66.4 us (11%)
  other arithmetic  21.2 us (4%)
  between operations  17.6 us (3%)
    reduce_scatter x1, waiting for transfers between devices, per_device(): lax.psum_scatter(jnp.concatenate([gate_term, up_term], axis=1), 'row', sc...  438 us
    all_gather x1, waiting for transfers between devices, per_device(): right_all = lax.all_gather(right_chosen, 'row', axis=1, tiled=True)  42.2 us
    dot_general x1, matrix products, merge_panel(): jnp.dot(left_panel, right_panel, preferred_element_type=jnp.float32)  23.1 us
    concatenate x1, other arithmetic, per_device(): jnp.concatenate([gate_term, up_term], axis=1)  20.3 us
    dot_general x1, matrix products, per_device(): lax.dot_general(up_weight, entire_result, contract, preferred_element_typ...  19.4 us
    dot_general x1, matrix products, per_device(): lax.dot_general(gate_merged, entire_result, contract, preferred_element_t...  19.1 us
  transfers between devices with their start and end apart: 3, of which 3 were waited for; matrix products, arithmetic and copies ran while one was open for 14% of the time, Pallas kernels for 0%

commit v1 on v0

v1 whole, which is shorter than its diff:
```python
import functools

import jax
import jax.numpy as jnp
from jax import lax
from jax.experimental import pallas as pl
from jax.experimental.pallas import tpu as pltpu
from jax.sharding import PartitionSpec as P


def merge_panel(weight, left_panel, right_panel):
    update = jnp.dot(left_panel, right_panel, preferred_element_type=jnp.float32)
    return (weight.astype(jnp.float32) + update).astype(jnp.bfloat16)


def choose(index, values):
    result = jnp.int32(values[-1])
    for at in range(len(values) - 2, -1, -1):
        result = jnp.where(index == at, jnp.int32(values[at]), result)
    return result


def chunks(width, step):
    return [(at, min(step, width - at)) for at in range(0, width, step)]


def scatter_kernel(
    line, tok_ref, up_ref, gate_ref, out_ref,
    wbuf, send_x, recv_x, own, recv_z,
    wsem, sx_sem, rx_sem, sz_sem, rz_sem,
):
    tokens, block = send_x.shape[1:]
    row = lax.axis_index("row")
    z = row // 2
    x = row % 2
    partner = z * 2 + (1 - x)
    terms = (up_ref, gate_ref)
    steps = 2 * line
    slots = wbuf.shape[0]
    orders = [sorted(range(line), key=lambda d: (-abs(d - at), d)) for at in range(line)]
    zd = [choose(z, [orders[at][j] for at in range(line)]) for j in range(line)]

    def tile_copy(index):
        step, mine = index // 2, index % 2
        column = zd[step % line] * 2 + (x if mine else 1 - x)
        source = terms[step // line].at[:, pl.ds(pl.multiple_of(column * block, 128), block)]
        return pltpu.make_async_copy(source, wbuf.at[index % slots], wsem.at[index % slots])

    for index in range(slots):
        tile_copy(index).start()

    barrier = pltpu.get_barrier_semaphore()
    pl.semaphore_signal(barrier, inc=1, device_id={"row": partner})

    @pl.when(z > 0)
    def _():
        pl.semaphore_signal(barrier, inc=1, device_id={"row": row - 2})

    @pl.when(z < line - 1)
    def _():
        pl.semaphore_signal(barrier, inc=1, device_id={"row": row + 2})

    pl.semaphore_wait(barrier, 1 + jnp.where(z > 0, 1, 0) + jnp.where(z < line - 1, 1, 0))

    def multiply(index, store):
        tile_copy(index).wait()
        slot = index % slots
        whole = block // 256

        def piece(columns):
            store(columns, jnp.dot(
                tok_ref[...], wbuf[slot, :, columns], preferred_element_type=jnp.float32
            ))

        @pl.loop(0, whole)
        def _(at):
            piece(pl.ds(pl.multiple_of(at * 256, 256), 256))

        if block % 256:
            piece(pl.ds(whole * 256, block % 256))
        if index + slots < 2 * steps:
            tile_copy(index + slots).start()

    def x_copy(step):
        return pltpu.make_async_remote_copy(
            src_ref=send_x.at[step], dst_ref=recv_x.at[step],
            send_sem=sx_sem.at[step], recv_sem=rx_sem.at[step],
            device_id={"row": partner},
        )

    def z_copy(step):
        term, j = step // line, step % line
        up = zd[j] > z
        target = jnp.where(up, row + 2, row - 2)
        at_end = jnp.logical_and(jnp.logical_not(up), zd[j] == z - 1)
        slot = term * (line + 1) + jnp.where(at_end, line, zd[j])
        return pltpu.make_async_remote_copy(
            src_ref=recv_x.at[step], dst_ref=recv_z.at[slot],
            send_sem=sz_sem.at[step], recv_sem=rz_sem.at[slot],
            device_id={"row": target},
        )

    def wait_z(slot):
        pltpu.make_async_remote_copy(
            src_ref=recv_z.at[slot], dst_ref=recv_z.at[slot],
            send_sem=sz_sem.at[0], recv_sem=rz_sem.at[slot],
            device_id={"row": partner},
        ).wait_recv()

    def produce(step):
        def to_send(columns, value):
            send_x[step, :, columns] = value.astype(jnp.bfloat16)

        def to_own(columns, value):
            own[step, :, columns] = value

        multiply(2 * step, to_send)
        x_copy(step).start()
        multiply(2 * step + 1, to_own)

    def add_rows(step, slot):
        @pl.loop(0, tokens // 16)
        def _(at):
            rows = pl.ds(pl.multiple_of(at * 16, 16), 16)
            own[step, rows, :] = own[step, rows, :] + recv_z[slot, rows, :].astype(jnp.float32)

    def finish(step):
        term, j = step // line, step % line
        if j < line - 1:
            inner = jnp.logical_or(
                jnp.logical_and(zd[j] > z, z > 0), jnp.logical_and(zd[j] < z, z < line - 1)
            )
            slot = term * (line + 1) + zd[j]

            @pl.when(inner)
            def _():
                wait_z(slot)
                add_rows(step, slot)

            x_copy(step).wait_recv()

            @pl.loop(0, tokens // 16)
            def _(at):
                rows = pl.ds(pl.multiple_of(at * 16, 16), 16)
                total = own[step, rows, :] + recv_x[step, rows, :].astype(jnp.float32)
                recv_x[step, rows, :] = total.astype(jnp.bfloat16)

            z_copy(step).start()
        else:
            x_copy(step).wait_recv()

            @pl.when(z > 0)
            def _():
                slot = term * (line + 1) + z
                wait_z(slot)
                add_rows(step, slot)

            @pl.when(z < line - 1)
            def _():
                slot = term * (line + 1) + line
                wait_z(slot)
                add_rows(step, slot)

            @pl.loop(0, tokens // 16)
            def _(at):
                rows = pl.ds(pl.multiple_of(at * 16, 16), 16)
                out_ref[term, rows, :] = own[step, rows, :] + recv_x[step, rows, :].astype(jnp.float32)

    for step in range(line):
        produce(step)
    done = 0
    for step in range(line, steps):
        finish(done)
        done += 1
        produce(step)
    for step in range(done, steps):
        finish(step)
    for step in range(steps):
        x_copy(step).wait_send()
        if step % line < line - 1:
            z_copy(step).wait_send()


def reduce_terms(tokens, up_weight, gate_weight, rows):
    count, width = tokens.shape
    block = up_weight.shape[1] // rows
    line = rows // 2
    steps = 2 * line
    return pl.pallas_call(
        functools.partial(scatter_kernel, line),
        out_shape=jax.ShapeDtypeStruct((2, count, block), jnp.float32),
        in_specs=[
            pl.BlockSpec(memory_space=pltpu.VMEM),
            pl.BlockSpec(memory_space=pl.ANY),
            pl.BlockSpec(memory_space=pl.ANY),
        ],
        out_specs=pl.BlockSpec(memory_space=pltpu.VMEM),
        scratch_shapes=[
            pltpu.VMEM((3, width, block), jnp.bfloat16),
            pltpu.VMEM((steps, count, block), jnp.bfloat16),
            pltpu.VMEM((steps, count, block), jnp.bfloat16),
            pltpu.VMEM((steps, count, block), jnp.float32),
            pltpu.VMEM((2 * (line + 1), count, block), jnp.bfloat16),
            pltpu.SemaphoreType.DMA((3,)),
            pltpu.SemaphoreType.DMA((steps,)),
            pltpu.SemaphoreType.DMA((steps,)),
            pltpu.SemaphoreType.DMA((steps,)),
            pltpu.SemaphoreType.DMA((2 * (line + 1),)),
        ],
        compiler_params=pltpu.CompilerParams(
            collective_id=0, has_side_effects=True, vmem_limit_bytes=56 * 2**20
        ),
        cost_estimate=pl.CostEstimate(
            flops=4 * count * width * block * rows,
            bytes_accessed=4 * width * block * rows,
            transcendentals=0,
        ),
    )(tokens, up_weight, gate_weight)


def per_device(tokens, gate_weight, up_weight, gate_up_left, gate_up_right, adapter_ids):
    rank = gate_up_right.shape[2]
    rows = lax.axis_size("row")
    old_id = adapter_ids[0]
    new_id = adapter_ids[1]
    incoming_left = gate_up_left[new_id]
    outgoing_left = gate_up_left[old_id]
    gate_left_panel = jnp.concatenate(
        [incoming_left[:, :rank], -outgoing_left[:, :rank]], axis=1
    )
    right_chosen = jnp.concatenate([gate_up_right[new_id, 0], gate_up_right[old_id, 0]], axis=0)
    all_tokens = lax.all_gather(tokens, "col", axis=0, tiled=True)
    right_all = lax.all_gather(right_chosen, "row", axis=1, tiled=True)
    gate_merged = merge_panel(gate_weight, gate_left_panel, right_all)
    scale = float(all_tokens.shape[1] * rows) ** (-0.5)
    count = all_tokens.shape[0]
    block = up_weight.shape[1] // rows
    if rows == 8 and block % 128 == 0 and count % 16 == 0:
        panels = jnp.concatenate([gate_left_panel, incoming_left[:, rank:]], axis=1)
        low = lax.psum(
            jnp.dot(all_tokens, panels, preferred_element_type=jnp.float32), "row"
        )
        sums = reduce_terms(all_tokens, up_weight, gate_weight, rows)
        gate_low = jnp.dot(
            low[:, : 2 * rank], right_chosen.astype(jnp.float32),
            precision=lax.Precision.HIGHEST, preferred_element_type=jnp.float32,
        )
        gate_value = (sums[1] + gate_low) * scale
        up_base = sums[0] * scale
        low_term = (low[:, 2 * rank :] * scale).astype(jnp.bfloat16)
    else:
        low = lax.psum(
            jnp.dot(all_tokens, incoming_left[:, rank:], preferred_element_type=jnp.float32), "row"
        )
        low_term = (low * scale).astype(jnp.bfloat16)
        contract = (((0,), (1,)), ((), ()))
        gate_term = lax.dot_general(
            gate_merged, all_tokens, contract, preferred_element_type=jnp.float32
        )
        up_term = lax.dot_general(
            up_weight, all_tokens, contract, preferred_element_type=jnp.float32
        )
        sums = lax.psum_scatter(
            jnp.concatenate([gate_term, up_term], axis=1), "row", scatter_dimension=0, tiled=True
        )
        gate_value = sums[:, :count].T * scale
        up_base = sums[:, count:].T * scale
    up_value = up_base + jnp.dot(
        low_term, gate_up_right[new_id, 1], preferred_element_type=jnp.float32
    )
    hidden = (jax.nn.silu(gate_value) * up_value).astype(jnp.bfloat16)
    return (gate_merged, hidden)


def solution(mesh):
    return jax.shard_map(
        per_device,
        mesh=mesh,
        in_specs=(
            P(("groups", "col"), "row"),
            P(("groups", "row"), "col"),
            P("row", "col"),
            P(None, "row", None),
            P(None, None, None, ("col", "row")),
            P("groups"),
        ),
        out_specs=(P(("groups", "row"), "col"), P("groups", ("col", "row"))),
        check_vma=False,
    )
```

time: 599 us -> 249 us (0.42)
  waiting for transfers between devices: 488 us -> 0.06 us
  Pallas kernels: 0 us -> 191 us
  matrix products: 66.4 us -> 30 us
  other arithmetic: 21.2 us -> 0.92 us
    reduce_scatter x1 -> x0, waiting for transfers between devices: 438 us -> none  [per_device(): lax.psum_scatter(jnp.concatenate([gate_term, up_term], axis=1), 'row', sc...]
    pallas_call x0 -> x1, Pallas kernels: none -> 191 us  [reduce_terms(): pl.pallas_call(functools.partial(scatter_kernel, line), out_shape=jax.Sha...]
    all_gather x1, waiting for transfers between devices: 42.2 us -> 0.01 us  [per_device(): right_all = lax.all_gather(right_chosen, 'row', axis=1, tiled=True)]
    dot_general x4 -> x3, matrix products: 43.3 us -> 6.69 us  [the longest x1 2.81 us: per_device(): jnp.dot(low[:, :2 * rank], right_chosen.astype(jnp.float32), precision=la...]
    concatenate x1 -> x0, other arithmetic: 20.3 us -> none  [per_device(): jnp.concatenate([gate_term, up_term], axis=1)]
    psum x1, waiting for transfers between devices: 8.01 us -> 0.02 us  [per_device(): lax.psum(jnp.dot(all_tokens, panels, preferred_element_type=jnp.float32),...]
  transfers between devices with their start and end apart: 3 -> 2, of which waited for: 3 -> 0; matrix products, arithmetic and copies ran while one was open for 14% -> 3% of each run, Pallas kernels for 0% -> 77%
where the time goes in v1:
time: 249 us; the launch traced here: 247 us
  Pallas kernels  191 us (77%)
  matrix products  30 us (12%)
  between operations  17.8 us (7%)
  local copies, waits for them, and re-layouts  4.97 us (2%)
    pallas_call x1, Pallas kernels, reduce_terms(): pl.pallas_call(functools.partial(scatter_kernel, line), out_shape=jax.Sha...  191 us
    dot_general x1, matrix products, merge_panel(): jnp.dot(left_panel, right_panel, preferred_element_type=jnp.float32)  23.3 us
  transfers between devices with their start and end apart: 2, of which 0 were waited for; matrix products, arithmetic and copies ran while one was open for 3% of the time, Pallas kernels for 77%

profile of v1, /device:TPU:0, one launch (start us, length us, event | category | flops | bytes accessed | tf_op | source)
XLA Modules:
  0.0 247.0 jit_solution(13348842309278728722)
XLA Ops:
  7.2 0.0 all-reduce.2.cloned.1.call-start
  7.2 1.3 fusion.23
  10.9 2.5 %all_gather.7.tok_ref = bf16[256,1024]{1,0:T(8,128)(2,1)S(1)} all-gather(bf16[128,1024]{1,0:T(8,128)(2,1)} %param.6), channel_id=1, replica_groups=mesh['groups'=2,'row'=8,'col'=2] {'col'}, dimensions={0}, use_global_device_ids=true | all-gather | bytes 786432 | tf_op jit(solution)/shard_map/all_gather | solution.py:232
  13.4 0.0 copy-start.1
  14.6 1.1 dynamic-slice_bitcast_fusion.1
  15.7 0.1 fusion.22
  15.9 0.0 copy-start.4
  15.9 0.0 copy-start.5
  15.9 0.7 copy-done.4
  16.6 0.1 copy-done.5
  16.6 1.3 convolution_bitcast_fusion
  17.9 0.0 copy-done.1
  17.9 0.0 all-reduce.2.cloned.1.call-update
  18.0 0.0 all-gather.2.cloned.1.call-start
  18.0 1.1 dynamic-slice_bitcast_fusion.3
  19.1 0.0 copy-start.2
  19.1 0.0 copy-start.3
  19.1 0.7 copy-done.2
  19.8 0.1 copy-done.3
  19.8 0.8 pad_maximum_fusion
  20.6 0.0 all-gather.2.cloned.1.call-update
  20.6 190.8 %shard_map.77 = f32[2,256,1664]{2,1,0:T(8,128)} custom-call(bf16[256,1024]{1,0:T(8,128)(2,1)} %copy-done.1, bf16[1024,13312]{1,0:T(8,128)(2,1)} %up_ref.1, bf16[1024,13312]{1,0:T(8,128)(2,1)} %gate_ref.1), custom_call_target="tpu_custom_call" | custom-call | flops 13958643712 | bytes 54525952 | tf_op jit(solution)/shard_map/pallas_call | solution.py:189
  211.4 0.0 copy-start
  211.4 0.0 all-reduce.2.cloned.1.call-done
  211.4 2.8 %fusion.1 = f32[256,1664]{1,0:T(8,128)S(1)} fusion(f32[2,256,1664]{2,1,0:T(8,128)} %shard_map.77, f32[256,192]{0,1:T(8,128)} %all-reduce.2.cloned.1.call-done, bf16[64,1664]{1,0:T(8,128)(2,1)} %copy-done.3, bf16[64,1664]{1,0:T(8,128)(2,1)} %copy-done.2), kind=kOutput, calls=%fused_computation.4 | convolution fusion | flops 656015360 | bytes 3964928 | tf_op jit(solution)/shard_map/dot_general | solution.py:244
  214.3 0.0 copy-done
  214.3 2.6 %fusion.2 = bf16[256,1664]{1,0:T(8,128)(2,1)} fusion(f32[2,256,1664]{2,1,0:T(8,128)S(1)} %copy-done, f32[256,1664]{1,0:T(8,128)S(1)} %fusion.1, bf16[4,2,64,1664]{3,2,1,0:T(8,128)(2,1)} %param.10, s32[]{:T(128)S(6)} %select_n.4, f32[256,192]{0,1:T(8,128)} %all-reduce.2.cloned.1.call-done), kind=kOutput, calls=%fused_computation.5 | convolution fusion | flops 57966592 | bytes 4538372 | tf_op jit(solution)/shard_map/dot_general | solution.py:268
  216.9 0.0 all-gather.2.cloned.1.call-done
  216.9 23.3 %add_convert_fusion = bf16[1024,13312]{1,0:T(8,128)(2,1)} fusion(bf16[1024,13312]{1,0:T(8,128)(2,1)} %gate_ref.1, bf16[128,13312]{1,0:T(8,128)(2,1)} %all-gather.2.cloned.1.call-done, bf16[1024,64]{1,0:T(8,128)(2,1)} %copy-done.5, bf16[1024,64]{1,0:T(8,128)(2,1)} %copy-done.4), kind=kOutput, calls=%fused_computation | convolution fusion | flops 3531079680 | bytes 58195968 | tf_op jit(solution)/shard_map/dot_general | solution.py:12
Async XLA Ops:
  7.2 204.3 %all-reduce.2.cloned.1.call-start = ((), (), s32[]{:S(2)}) async-start(), calls=%async_computation.1 | async-start | bytes 393216 | tf_op jit(solution)/shard_map/psum | solution.py:240
  13.4 4.5 %copy-start.1 = (bf16[256,1024]{1,0:T(8,128)(2,1)}, bf16[256,1024]{1,0:T(8,128)(2,1)S(1)}, u32[]{:S(2)}) copy-start(bf16[256,1024]{1,0:T(8,128)(2,1)S(1)} %all_gather.7.tok_ref) | copy-start | bytes 1572868
  15.9 0.7 copy-start.4
  15.9 0.8 copy-start.5
  18.0 198.9 %all-gather.2.cloned.1.call-start = ((), (), s32[]{:S(2)}) async-start(), calls=%async_computation | async-start | bytes 3833856 | tf_op jit(solution)/shard_map/all_gather | solution.py:233
  19.1 0.7 copy-start.2
  19.1 0.7 copy-start.3
  211.4 2.9 %copy-start = (f32[2,256,1664]{2,1,0:T(8,128)S(1)}, f32[2,256,1664]{2,1,0:T(8,128)}, u32[]{:S(2)}) copy-start(f32[2,256,1664]{2,1,0:T(8,128)} %shard_map.77) | copy-start | bytes 10223620
Sparse Core Ops, SparseCore 0:
  18.1 73.6 all-reduce.1
  94.8 93.8 all-gather.1

commit v2 on v1

--- a/solution.py
+++ b/solution.py
@@ -20,14 +20,11 @@
     return result
 
 
-def chunks(width, step):
-    return [(at, min(step, width - at)) for at in range(0, width, step)]
-
-
 def scatter_kernel(
-    line, tok_ref, up_ref, gate_ref, out_ref,
+    line, tok_ref, up_ref, gate_ref, right_ref, out_ref, hop_ref, panel_ref,
     wbuf, send_x, recv_x, own, recv_z,
     wsem, sx_sem, rx_sem, sz_sem, rz_sem,
+    own_sem, pair_sem, up_sem, down_sem, panel_sem,
 ):
     tokens, block = send_x.shape[1:]
     row = lax.axis_index("row")
@@ -62,6 +59,63 @@
 
     pl.semaphore_wait(barrier, 1 + jnp.where(z > 0, 1, 0) + jnp.where(z < line - 1, 1, 0))
 
+    def panel_at(first, width):
+        return panel_ref.at[:, pl.ds(pl.multiple_of(first * block, 128), width * block)]
+
+    own_panel = pltpu.make_async_copy(right_ref, panel_at(row, 1), own_sem)
+    own_panel.start()
+
+    def pair_copy(owner):
+        return pltpu.make_async_remote_copy(
+            src_ref=right_ref, dst_ref=panel_at(owner, 1),
+            send_sem=pair_sem.at[0], recv_sem=pair_sem.at[1],
+            device_id={"row": partner},
+        )
+
+    pair_copy(row).start()
+
+    def panel_copy(owner, upward):
+        sems = up_sem if upward else down_sem
+        return pltpu.make_async_remote_copy(
+            src_ref=panel_at(owner * 2, 2), dst_ref=panel_at(owner * 2, 2),
+            send_sem=sems.at[owner], recv_sem=panel_sem.at[owner],
+            device_id={"row": row + 2 if upward else row - 2},
+        )
+
+    def gather(hop):
+        if hop == 0:
+            own_panel.wait()
+            pair_copy(partner).wait_recv()
+
+        @pl.when(z - hop >= 0)
+        def _():
+            if hop:
+                panel_copy(z - hop, True).wait_recv()
+
+            @pl.when(z < line - 1)
+            def _():
+                panel_copy(z - hop, True).start()
+
+        @pl.when(z + hop < line)
+        def _():
+            if hop:
+                panel_copy(z + hop, False).wait_recv()
+
+            @pl.when(z > 0)
+            def _():
+                panel_copy(z + hop, False).start()
+
+    def gather_end():
+        pair_copy(row).wait_send()
+        for hop in range(line):
+            @pl.when(jnp.logical_and(z - hop >= 0, z < line - 1))
+            def _():
+                panel_copy(z - hop, True).wait_send()
+
+            @pl.when(jnp.logical_and(z + hop < line, z > 0))
+            def _():
+                panel_copy(z + hop, False).wait_send()
+
     def multiply(index, store):
         tile_copy(index).wait()
         slot = index % slots
@@ -118,6 +172,9 @@
         x_copy(step).start()
         multiply(2 * step + 1, to_own)
 
+    def last_hop(j):
+        return jnp.logical_or(zd[j] == z + 1, zd[j] == z - 1)
+
     def add_rows(step, slot):
         @pl.loop(0, tokens // 16)
         def _(at):
@@ -145,21 +202,36 @@
                 total = own[step, rows, :] + recv_x[step, rows, :].astype(jnp.float32)
                 recv_x[step, rows, :] = total.astype(jnp.bfloat16)
 
-            z_copy(step).start()
+            if term == 0:
+                z_copy(step).start()
+            else:
+                @pl.when(last_hop(j))
+                def _():
+                    side = jnp.where(zd[j] > z, 0, 1)
+
+                    @pl.loop(0, tokens // 16)
+                    def _(at):
+                        rows = pl.ds(pl.multiple_of(at * 16, 16), 16)
+                        hop_ref[side, rows, :] = recv_x[step, rows, :]
+
+                @pl.when(jnp.logical_not(last_hop(j)))
+                def _():
+                    z_copy(step).start()
         else:
             x_copy(step).wait_recv()
 
-            @pl.when(z > 0)
-            def _():
-                slot = term * (line + 1) + z
-                wait_z(slot)
-                add_rows(step, slot)
-
-            @pl.when(z < line - 1)
-            def _():
-                slot = term * (line + 1) + line
-                wait_z(slot)
-                add_rows(step, slot)
+            if term == 0:
+                @pl.when(z > 0)
+                def _():
+                    slot = term * (line + 1) + z
+                    wait_z(slot)
+                    add_rows(step, slot)
+
+                @pl.when(z < line - 1)
+                def _():
+                    slot = term * (line + 1) + line
+                    wait_z(slot)
+                    add_rows(step, slot)
 
             @pl.loop(0, tokens // 16)
             def _(at):
@@ -168,33 +240,51 @@
 
     for step in range(line):
         produce(step)
+        if step == 0:
+            gather(0)
     done = 0
     for step in range(line, steps):
         finish(done)
         done += 1
         produce(step)
+        if done < line:
+            gather(done)
     for step in range(done, steps):
         finish(step)
     for step in range(steps):
         x_copy(step).wait_send()
-        if step % line < line - 1:
+        if step < line - 1:
             z_copy(step).wait_send()
-
-
-def reduce_terms(tokens, up_weight, gate_weight, rows):
+        elif line <= step < steps - 1:
+            @pl.when(jnp.logical_not(last_hop(step - line)))
+            def _():
+                z_copy(step).wait_send()
+    gather_end()
+
+
+def reduce_terms(tokens, up_weight, gate_weight, right, rows):
     count, width = tokens.shape
     block = up_weight.shape[1] // rows
     line = rows // 2
     steps = 2 * line
     return pl.pallas_call(
         functools.partial(scatter_kernel, line),
-        out_shape=jax.ShapeDtypeStruct((2, count, block), jnp.float32),
+        out_shape=(
+            jax.ShapeDtypeStruct((2, count, block), jnp.float32),
+            jax.ShapeDtypeStruct((2, count, block), jnp.bfloat16),
+            jax.ShapeDtypeStruct((right.shape[0], rows * block), jnp.bfloat16),
+        ),
         in_specs=[
             pl.BlockSpec(memory_space=pltpu.VMEM),
             pl.BlockSpec(memory_space=pl.ANY),
             pl.BlockSpec(memory_space=pl.ANY),
+            pl.BlockSpec(memory_space=pl.ANY),
         ],
-        out_specs=pl.BlockSpec(memory_space=pltpu.VMEM),
+        out_specs=(
+            pl.BlockSpec(memory_space=pltpu.VMEM),
+            pl.BlockSpec(memory_space=pltpu.VMEM),
+            pl.BlockSpec(memory_space=pl.ANY),
+        ),
         scratch_shapes=[
             pltpu.VMEM((3, width, block), jnp.bfloat16),
             pltpu.VMEM((steps, count, block), jnp.bfloat16),
@@ -206,6 +296,11 @@
             pltpu.SemaphoreType.DMA((steps,)),
             pltpu.SemaphoreType.DMA((steps,)),
             pltpu.SemaphoreType.DMA((2 * (line + 1),)),
+            pltpu.SemaphoreType.DMA,
+            pltpu.SemaphoreType.DMA((2,)),
+            pltpu.SemaphoreType.DMA((line,)),
+            pltpu.SemaphoreType.DMA((line,)),
+            pltpu.SemaphoreType.DMA((line,)),
         ],
         compiler_params=pltpu.CompilerParams(
             collective_id=0, has_side_effects=True, vmem_limit_bytes=56 * 2**20
@@ -215,7 +310,7 @@
             bytes_accessed=4 * width * block * rows,
             transcendentals=0,
         ),
-    )(tokens, up_weight, gate_weight)
+    )(tokens, up_weight, gate_weight, right)
 
 
 def per_device(tokens, gate_weight, up_weight, gate_up_left, gate_up_right, adapter_ids):
@@ -230,8 +325,6 @@
     )
     right_chosen = jnp.concatenate([gate_up_right[new_id, 0], gate_up_right[old_id, 0]], axis=0)
     all_tokens = lax.all_gather(tokens, "col", axis=0, tiled=True)
-    right_all = lax.all_gather(right_chosen, "row", axis=1, tiled=True)
-    gate_merged = merge_panel(gate_weight, gate_left_panel, right_all)
     scale = float(all_tokens.shape[1] * rows) ** (-0.5)
     count = all_tokens.shape[0]
     block = up_weight.shape[1] // rows
@@ -240,15 +333,23 @@
         low = lax.psum(
             jnp.dot(all_tokens, panels, preferred_element_type=jnp.float32), "row"
         )
-        sums = reduce_terms(all_tokens, up_weight, gate_weight, rows)
+        sums, hops, right_all = reduce_terms(
+            all_tokens, up_weight, gate_weight, right_chosen, rows
+        )
+        below = lax.ppermute(hops[0], "row", [(at, at + 2) for at in range(rows - 2)])
+        above = lax.ppermute(hops[1], "row", [(at + 2, at) for at in range(rows - 2)])
+        gate_merged = merge_panel(gate_weight, gate_left_panel, right_all)
         gate_low = jnp.dot(
             low[:, : 2 * rank], right_chosen.astype(jnp.float32),
             precision=lax.Precision.HIGHEST, preferred_element_type=jnp.float32,
         )
-        gate_value = (sums[1] + gate_low) * scale
+        gate_sum = sums[1] + below.astype(jnp.float32) + above.astype(jnp.float32)
+        gate_value = (gate_sum + gate_low) * scale
         up_base = sums[0] * scale
         low_term = (low[:, 2 * rank :] * scale).astype(jnp.bfloat16)
     else:
+        right_all = lax.all_gather(right_chosen, "row", axis=1, tiled=True)
+        gate_merged = merge_panel(gate_weight, gate_left_panel, right_all)
         low = lax.psum(
             jnp.dot(all_tokens, incoming_left[:, rank:], preferred_element_type=jnp.float32), "row"
         )

time: 249 us -> 243 us (0.976)
  Pallas kernels: 191 us -> 167 us
  starting transfers between devices: 0.08 us -> 17.9 us
    pallas_call x1, Pallas kernels: 191 us -> 167 us  [reduce_terms(): pl.pallas_call(functools.partial(scatter_kernel, line), out_shape=(jax.Sh...]
    ppermute x0 -> x2, starting transfers between devices: none -> 17.9 us  [the longest x1 16.4 us: per_device(): lax.ppermute(hops[0], 'row', [(at, at + 2) for at in range(rows - 2)])]
    squeeze x0 -> x1, local copies, waits for them, and re-layouts: none -> 2.97 us  [per_device(): hops[0]]
  transfers between devices with their start and end apart: 2 -> 3, of which waited for: 0 -> 0; matrix products, arithmetic and copies ran while one was open for 3% -> 12% of each run, Pallas kernels for 77% -> 69%
where the time goes in v2:
time: 243 us
  Pallas kernels  167 us (69%)
  matrix products  30 us (12%)
  between operations  18 us (7%)
  starting transfers between devices  17.9 us (7%)
  local copies, waits for them, and re-layouts  7.32 us (3%)
    pallas_call x1, Pallas kernels, reduce_terms(): pl.pallas_call(functools.partial(scatter_kernel, line), out_shape=(jax.Sh...  167 us
    dot_general x1, matrix products, merge_panel(): jnp.dot(left_panel, right_panel, preferred_element_type=jnp.float32)  22.2 us
    ppermute x1, starting transfers between devices, per_device(): lax.ppermute(hops[0], 'row', [(at, at + 2) for at in range(rows - 2)])  16.4 us
  transfers between devices with their start and end apart: 3, of which 0 were waited for; matrix products, arithmetic and copies ran while one was open for 12% of the time, Pallas kernels for 69%

profile of v2, /device:TPU:0, one launch (start us, length us, event | category | flops | bytes accessed | tf_op | source)
XLA Modules:
  0.0 243.1 jit_solution(8880150118812741184)
XLA Ops:
  7.2 0.0 copy-start.6
  7.2 0.0 all-reduce.2.cloned.1.call-start
  7.2 1.3 fusion.24
  12.4 1.1 dynamic-slice_bitcast_fusion.1
  13.5 0.0 copy-start.4
  13.5 0.1 fusion.23
  13.7 0.0 copy-done.6
  13.7 0.0 copy-start.5
  13.7 2.3 all_gather.3.tok_ref
  16.0 0.0 copy-start.1
  16.0 0.0 copy-done.4
  16.0 0.0 copy-done.5
  16.0 1.3 convolution_bitcast_fusion
  17.3 0.0 all-reduce.2.cloned.1.call-update
  17.3 1.1 dynamic-slice_bitcast_fusion.3
  18.4 0.0 copy-start.2
  18.4 0.0 copy-start.3
  18.4 0.7 copy-done.2
  19.0 0.1 copy-done.3
  19.1 0.8 pad_maximum_fusion.right_ref
  19.9 0.0 copy-done.1
  19.9 166.7 %shard_map.77 = (f32[2,256,1664]{2,1,0:T(8,128)}, bf16[2,256,1664]{2,1,0:T(8,128)(2,1)}, bf16[128,13312]{1,0:T(8,128)(2,1)}) custom-call(bf16[256,1024]{1,0:T(8,128)(2,1)} %copy-done.1, bf16[1024,13312]{1,0:T(8,128)(2,1)} %up_ref.1, bf16[1024,13312]{1,0:T(8,128)(2,1)} %gate_ref.1, bf16[128,1664]{1,0:T(8,128)(2,1)} %pad_maximum_fusion.right_ref), custom_call_target="tpu_custom_call" | custom-call | flops 13958643712 | bytes 54525952 | tf_op jit(solution)/shard_map/pallas_call | solution.py:270
  186.6 0.0 copy-start
  186.6 3.0 %slice_bitcast_fusion.1 = (bf16[256,1664]{1,0:T(8,128)(2,1)}, bf16[256,1664]{1,0:T(8,128)(2,1)}) fusion(bf16[2,256,1664]{2,1,0:T(8,128)(2,1)} %get-tuple-element.7), kind=kLoop, calls=%fused_computation.9 | loop fusion | bytes 3407872 | tf_op jit(solution)/shard_map/squeeze | solution.py:339
  189.6 16.4 %collective-permute-start = (bf16[256,1664]{1,0:T(8,128)(2,1)}, bf16[256,1664]{1,0:T(8,128)(2,1)}, u32[]{:S(2)}, u32[]{:S(2)}) collective-permute-start(bf16[256,1664]{1,0:T(8,128)(2,1)} %get-tuple-element.8), channel_id=1, source_target_pairs={{0,4},{2,6},{4,8},{6,10},{8,12},{10,14},{1,5},{3,7},{5,9},{7,11},{... | collective-permute-start | bytes 2555912 | tf_op jit(solution)/shard_map/ppermute | solution.py:339
  206.0 1.5 collective-permute-start.1
  207.5 0.0 copy-done
  207.5 22.2 %add_convert_fusion = bf16[1024,13312]{1,0:T(8,128)(2,1)} fusion(bf16[1024,13312]{1,0:T(8,128)(2,1)} %gate_ref.1, bf16[128,13312]{1,0:T(8,128)(2,1)S(1)} %copy-done, bf16[1024,64]{1,0:T(8,128)(2,1)} %copy-done.4, bf16[1024,64]{1,0:T(8,128)(2,1)} %copy-done.5), kind=kOutput, calls=%fused_computation | convolution fusion | flops 3531079680 | bytes 58195968 | tf_op jit(solution)/shard_map/dot_general | solution.py:12
  229.7 0.0 all-reduce.2.cloned.1.call-done
  229.7 2.0 fusion.13
  231.7 0.0 collective-permute-done
  231.7 0.0 collective-permute-done.1
  231.7 4.6 %multiply_convert_fusion = bf16[256,1664]{1,0:T(8,128)(2,1)} fusion(f32[256,1664]{1,0:T(8,128)S(1)} %fusion.13, bf16[256,1664]{1,0:T(8,128)(2,1)} %collective-permute-done.1, bf16[256,1664]{1,0:T(8,128)(2,1)} %collective-permute-done, f32[2,256,1664]{2,1,0:T(8,128)} %get-tuple-element.6, bf16[4,2,64,1664]{3,2,1,0:T(8,128)(2,1)} %param.10, s32[]{:T(128)S(6)} %select_n.4, ...), kind=kOutput, calls=%fused_computation.6 | convolution fusion | flops 60522496 | bytes 7946244 | tf_op jit(solution)/shard_map/dot_general | solution.py:369
  (1 shorter events, 0.0 us)
Async XLA Ops:
  7.2 6.5 %copy-start.6 = (bf16[128,1024]{1,0:T(8,128)(2,1)S(1)}, bf16[128,1024]{1,0:T(8,128)(2,1)}, u32[]{:S(2)}) copy-start(bf16[128,1024]{1,0:T(8,128)(2,1)} %param.6) | copy-start | bytes 786436
  7.2 222.5 %all-reduce.2.cloned.1.call-start = ((), (), s32[]{:S(2)}) async-start(), calls=%async_computation | async-start | bytes 393216 | tf_op jit(solution)/shard_map/psum | solution.py:333
  13.5 2.4 %copy-start.4 = (bf16[1024,64]{1,0:T(8,128)(2,1)}, bf16[1024,64]{1,0:T(8,128)(2,1)S(1)}, u32[]{:S(2)}) copy-start(bf16[1024,64]{1,0:T(8,128)(2,1)S(1)} %slice_negate_fusion) | copy-start | bytes 393220
  13.7 2.3 copy-start.5
  16.0 3.9 %copy-start.1 = (bf16[256,1024]{1,0:T(8,128)(2,1)}, bf16[256,1024]{1,0:T(8,128)(2,1)S(1)}, u32[]{:S(2)}) copy-start(bf16[256,1024]{1,0:T(8,128)(2,1)S(1)} %all_gather.3.tok_ref) | copy-start | bytes 1572868
  18.4 0.7 copy-start.2
  18.4 0.7 copy-start.3
  186.6 20.9 %copy-start = (bf16[128,13312]{1,0:T(8,128)(2,1)S(1)}, bf16[128,13312]{1,0:T(8,128)(2,1)}, u32[]{:S(2)}) copy-start(bf16[128,13312]{1,0:T(8,128)(2,1)} %get-tuple-element.5) | copy-start | bytes 10223620
  189.6 42.1 %collective-permute-start = (bf16[256,1664]{1,0:T(8,128)(2,1)}, bf16[256,1664]{1,0:T(8,128)(2,1)}, u32[]{:S(2)}, u32[]{:S(2)}) collective-permute-start(bf16[256,1664]{1,0:T(8,128)(2,1)} %get-tuple-element.8), channel_id=1, source_target_pairs={{0,4},{2,6},{4,8},{6,10},{8,12},{10,14},{1,5},{3,7},{5,9},{7,11},{... | collective-permute-start | bytes 2555912 | tf_op jit(solution)/shard_map/ppermute | solution.py:339
  206.0 25.7 %collective-permute-start.1 = (bf16[256,1664]{1,0:T(8,128)(2,1)}, bf16[256,1664]{1,0:T(8,128)(2,1)}, u32[]{:S(2)}, u32[]{:S(2)}) collective-permute-start(bf16[256,1664]{1,0:T(8,128)(2,1)} %get-tuple-element.9), channel_id=1, source_target_pairs={{4,0},{6,2},{8,4},{10,6},{12,8},{14,10},{5,1},{7,3},{9,5},{11,7},{... | collective-permute-start | bytes 2555912 | tf_op jit(solution)/shard_map/ppermute | solution.py:340
Sparse Core Ops, SparseCore 0:
  17.4 73.6 all-reduce.1

commit v3 on v2

--- a/solution.py
+++ b/solution.py
@@ -21,7 +21,8 @@
 
 
 def scatter_kernel(
-    line, tok_ref, up_ref, gate_ref, right_ref, out_ref, hop_ref, panel_ref,
+    line, tok_ref, up_ref, gate_ref, right_ref,
+    out_ref, up_hop_ref, down_hop_ref, pair_hop_ref, panel_ref,
     wbuf, send_x, recv_x, own, recv_z,
     wsem, sx_sem, rx_sem, sz_sem, rz_sem,
     own_sem, pair_sem, up_sem, down_sem, panel_sem,
@@ -168,9 +169,19 @@
         def to_own(columns, value):
             own[step, :, columns] = value
 
-        multiply(2 * step, to_send)
-        x_copy(step).start()
-        multiply(2 * step + 1, to_own)
+        def to_pair_hop(columns, value):
+            pair_hop_ref[:, columns] = value.astype(jnp.bfloat16)
+
+        def to_out(columns, value):
+            out_ref[1, :, columns] = value
+
+        if step < steps - 1:
+            multiply(2 * step, to_send)
+            x_copy(step).start()
+            multiply(2 * step + 1, to_own)
+        else:
+            multiply(2 * step, to_pair_hop)
+            multiply(2 * step + 1, to_out)
 
     def last_hop(j):
         return jnp.logical_or(zd[j] == z + 1, zd[j] == z - 1)
@@ -205,14 +216,19 @@
             if term == 0:
                 z_copy(step).start()
             else:
-                @pl.when(last_hop(j))
-                def _():
-                    side = jnp.where(zd[j] > z, 0, 1)
-
+                def keep(hop_ref):
                     @pl.loop(0, tokens // 16)
                     def _(at):
                         rows = pl.ds(pl.multiple_of(at * 16, 16), 16)
-                        hop_ref[side, rows, :] = recv_x[step, rows, :]
+                        hop_ref[rows, :] = recv_x[step, rows, :]
+
+                @pl.when(zd[j] == z + 1)
+                def _():
+                    keep(up_hop_ref)
+
+                @pl.when(zd[j] == z - 1)
+                def _():
+                    keep(down_hop_ref)
 
                 @pl.when(jnp.logical_not(last_hop(j)))
                 def _():
@@ -220,18 +236,17 @@
         else:
             x_copy(step).wait_recv()
 
-            if term == 0:
-                @pl.when(z > 0)
-                def _():
-                    slot = term * (line + 1) + z
-                    wait_z(slot)
-                    add_rows(step, slot)
-
-                @pl.when(z < line - 1)
-                def _():
-                    slot = term * (line + 1) + line
-                    wait_z(slot)
-                    add_rows(step, slot)
+            @pl.when(z > 0)
+            def _():
+                slot = term * (line + 1) + z
+                wait_z(slot)
+                add_rows(step, slot)
+
+            @pl.when(z < line - 1)
+            def _():
+                slot = term * (line + 1) + line
+                wait_z(slot)
+                add_rows(step, slot)
 
             @pl.loop(0, tokens // 16)
             def _(at):
@@ -249,13 +264,13 @@
         produce(step)
         if done < line:
             gather(done)
-    for step in range(done, steps):
+    for step in range(done, steps - 1):
         finish(step)
-    for step in range(steps):
+    for step in range(steps - 1):
         x_copy(step).wait_send()
         if step < line - 1:
             z_copy(step).wait_send()
-        elif line <= step < steps - 1:
+        elif step >= line:
             @pl.when(jnp.logical_not(last_hop(step - line)))
             def _():
                 z_copy(step).wait_send()
@@ -271,7 +286,9 @@
         functools.partial(scatter_kernel, line),
         out_shape=(
             jax.ShapeDtypeStruct((2, count, block), jnp.float32),
-            jax.ShapeDtypeStruct((2, count, block), jnp.bfloat16),
+            jax.ShapeDtypeStruct((count, block), jnp.bfloat16),
+            jax.ShapeDtypeStruct((count, block), jnp.bfloat16),
+            jax.ShapeDtypeStruct((count, block), jnp.bfloat16),
             jax.ShapeDtypeStruct((right.shape[0], rows * block), jnp.bfloat16),
         ),
         in_specs=[
@@ -281,6 +298,8 @@
             pl.BlockSpec(memory_space=pl.ANY),
         ],
         out_specs=(
+            pl.BlockSpec(memory_space=pltpu.VMEM),
+            pl.BlockSpec(memory_space=pltpu.VMEM),
             pl.BlockSpec(memory_space=pltpu.VMEM),
             pl.BlockSpec(memory_space=pltpu.VMEM),
             pl.BlockSpec(memory_space=pl.ANY),
@@ -333,17 +352,19 @@
         low = lax.psum(
             jnp.dot(all_tokens, panels, preferred_element_type=jnp.float32), "row"
         )
-        sums, hops, right_all = reduce_terms(
+        sums, up_hop, down_hop, pair_hop, right_all = reduce_terms(
             all_tokens, up_weight, gate_weight, right_chosen, rows
         )
-        below = lax.ppermute(hops[0], "row", [(at, at + 2) for at in range(rows - 2)])
-        above = lax.ppermute(hops[1], "row", [(at + 2, at) for at in range(rows - 2)])
+        below = lax.ppermute(up_hop, "row", [(at, at + 2) for at in range(rows - 2)])
+        above = lax.ppermute(down_hop, "row", [(at + 2, at) for at in range(rows - 2)])
+        beside = lax.ppermute(pair_hop, "row", [(at, at ^ 1) for at in range(rows)])
         gate_merged = merge_panel(gate_weight, gate_left_panel, right_all)
         gate_low = jnp.dot(
             low[:, : 2 * rank], right_chosen.astype(jnp.float32),
             precision=lax.Precision.HIGHEST, preferred_element_type=jnp.float32,
         )
-        gate_sum = sums[1] + below.astype(jnp.float32) + above.astype(jnp.float32)
+        gate_sum = sums[1] + beside.astype(jnp.float32)
+        gate_sum = gate_sum + below.astype(jnp.float32) + above.astype(jnp.float32)
         gate_value = (gate_sum + gate_low) * scale
         up_base = sums[0] * scale
         low_term = (low[:, 2 * rank :] * scale).astype(jnp.bfloat16)

time: 243 us -> 240 us (0.988)
  starting transfers between devices: 17.9 us -> 22.1 us
  Pallas kernels: 167 us -> 163 us
  local copies, waits for them, and re-layouts: 7.32 us -> 3.6 us
    pallas_call x1, Pallas kernels: 167 us -> 163 us  [reduce_terms(): pl.pallas_call(functools.partial(scatter_kernel, line), out_shape=(jax.Sh...]
    ppermute x2 -> x3, starting transfers between devices: 17.9 us -> 22 us  [the longest x1 18.4 us: per_device(): lax.ppermute(up_hop, 'row', [(at, at + 2) for at in range(rows - 2)])]
    squeeze x1 -> x0, local copies, waits for them, and re-layouts: 2.97 us -> none  [per_device(): hops[0]]
  transfers between devices with their start and end apart: 3 -> 4, of which waited for: 0 -> 0; matrix products, arithmetic and copies ran while one was open for 12% -> 11% of each run, Pallas kernels for 69% -> 68%
where the time goes in v3:
time: 240 us
  Pallas kernels  163 us (68%)
  matrix products  30.7 us (13%)
  starting transfers between devices  22.1 us (9%)
  between operations  18 us (8%)
  local copies, waits for them, and re-layouts  3.6 us (2%)
    pallas_call x1, Pallas kernels, reduce_terms(): pl.pallas_call(functools.partial(scatter_kernel, line), out_shape=(jax.Sh...  163 us
    dot_general x1, matrix products, merge_panel(): jnp.dot(left_panel, right_panel, preferred_element_type=jnp.float32)  23.2 us
    ppermute x1, starting transfers between devices, per_device(): lax.ppermute(up_hop, 'row', [(at, at + 2) for at in range(rows - 2)])  18.4 us
  transfers between devices with their start and end apart: 4, of which 0 were waited for; matrix products, arithmetic and copies ran while one was open for 11% of the time, Pallas kernels for 68%

profile of v3, /device:TPU:0, one launch (start us, length us, event | category | flops | bytes accessed | tf_op | source)
XLA Modules:
  0.0 240.0 jit_solution(10769906218738063595)
XLA Ops:
  7.2 0.0 copy-start.1
  7.2 0.0 all-reduce.2.cloned.1.call-start
  7.2 1.3 fusion.25
  12.4 1.1 dynamic-slice_bitcast_fusion.1
  13.5 0.1 fusion.24
  13.7 0.0 copy-done.1
  13.7 2.3 all_gather.3.tok_ref
  15.9 0.0 copy-start
  16.0 1.3 convolution_bitcast_fusion
  17.2 0.0 all-reduce.2.cloned.1.call-update
  17.3 1.1 dynamic-slice_bitcast_fusion.3
  18.3 0.8 pad_maximum_fusion.right_ref
  19.1 0.0 copy-done
  19.1 162.5 %shard_map.77 = (f32[2,256,1664]{2,1,0:T(8,128)}, bf16[256,1664]{1,0:T(8,128)(2,1)}, bf16[256,1664]{1,0:T(8,128)(2,1)}, bf16[256,1664]{1,0:T(8,128)(2,1)}, bf16[128,13312]{1,0:T(8,128)(2,1)}) custom-call(bf16[256,1024]{1,0:T(8,128)(2,1)} %copy-done, bf16[1024,13312]{1,0:T(8,128)(2,1)} %up_ref.1, bf16[1024,13312]{1,0:T(8,128)(2,1)} %gate_ref.1, ...), custom_call_target="tpu_custom_call" | custom-call | flops 13958643712 | bytes 54525952 | tf_op jit(solution)/shard_map/pallas_call | solution.py:285
  181.7 2.2 collective-permute-start
  183.8 18.4 %collective-permute-start.1 = (bf16[256,1664]{1,0:T(8,128)(2,1)}, bf16[256,1664]{1,0:T(8,128)(2,1)S(1)}, u32[]{:S(2)}, u32[]{:S(2)}) collective-permute-start(bf16[256,1664]{1,0:T(8,128)(2,1)} %get-tuple-element.10), channel_id=1, source_target_pairs={{0,4},{2,6},{4,8},{6,10},{8,12},{10,14},{1,5},{3,7},{5,9},{7,11},{... | collective-permute-start | bytes 2555912 | tf_op jit(solution)/shard_map/ppermute | solution.py:358
  202.2 1.5 collective-permute-start.2
  203.7 23.2 %add_convert_fusion = bf16[1024,13312]{1,0:T(8,128)(2,1)} fusion(bf16[1024,13312]{1,0:T(8,128)(2,1)} %gate_ref.1, bf16[128,13312]{1,0:T(8,128)(2,1)} %get-tuple-element.7, bf16[1024,64]{1,0:T(8,128)(2,1)S(1)} %slice_negate_fusion, bf16[1024,64]{1,0:T(8,128)(2,1)S(1)} %get-tuple-element.17), kind=kOutput, calls=%fused_computation | convolution fusion | flops 3531079680 | bytes 58195968 | tf_op jit(solution)/shard_map/dot_general | solution.py:12
  226.9 0.0 all-reduce.2.cloned.1.call-done
  226.9 1.8 fusion.14
  228.6 0.0 collective-permute-done
  228.7 0.0 collective-permute-done.1
  228.7 0.0 collective-permute-done.2
  228.7 4.4 %multiply_convert_fusion = bf16[256,1664]{1,0:T(8,128)(2,1)} fusion(f32[256,1664]{1,0:T(8,128)S(1)} %fusion.14, bf16[256,1664]{1,0:T(8,128)(2,1)} %collective-permute-done.2, bf16[256,1664]{1,0:T(8,128)(2,1)S(1)} %collective-permute-done.1, bf16[256,1664]{1,0:T(8,128)(2,1)S(1)} %collective-permute-done, f32[2,256,1664]{2,1,0:T(8,128)} %get-tuple-element.8, ...), kind=kOutput, calls=%fused_computation.7 | convolution fusion | flops 61374464 | bytes 8798212 | tf_op jit(solution)/shard_map/dot_general | solution.py:390
  (1 shorter events, 0.0 us)
Async XLA Ops:
  7.2 6.5 %copy-start.1 = (bf16[128,1024]{1,0:T(8,128)(2,1)S(1)}, bf16[128,1024]{1,0:T(8,128)(2,1)}, u32[]{:S(2)}) copy-start(bf16[128,1024]{1,0:T(8,128)(2,1)} %param.6) | copy-start | bytes 786436
  7.2 219.7 %all-reduce.2.cloned.1.call-start = ((), (), s32[]{:S(2)}) async-start(), calls=%async_computation | async-start | bytes 393216 | tf_op jit(solution)/shard_map/psum | solution.py:352
  15.9 3.2 %copy-start = (bf16[256,1024]{1,0:T(8,128)(2,1)}, bf16[256,1024]{1,0:T(8,128)(2,1)S(1)}, u32[]{:S(2)}) copy-start(bf16[256,1024]{1,0:T(8,128)(2,1)S(1)} %all_gather.3.tok_ref) | copy-start | bytes 1572868
  181.7 47.0 %collective-permute-start = (bf16[256,1664]{1,0:T(8,128)(2,1)}, bf16[256,1664]{1,0:T(8,128)(2,1)S(1)}, u32[]{:S(2)}, u32[]{:S(2)}) collective-permute-start(bf16[256,1664]{1,0:T(8,128)(2,1)} %get-tuple-element.9), channel_id=1, source_target_pairs={{0,2},{2,0},{4,6},{6,4},{8,10},{10,8},{12,14},{14,12},{1,3},{3,1},... | collective-permute-start | bytes 2555912 | tf_op jit(solution)/shard_map/ppermute | solution.py:360
  183.8 44.9 %collective-permute-start.1 = (bf16[256,1664]{1,0:T(8,128)(2,1)}, bf16[256,1664]{1,0:T(8,128)(2,1)S(1)}, u32[]{:S(2)}, u32[]{:S(2)}) collective-permute-start(bf16[256,1664]{1,0:T(8,128)(2,1)} %get-tuple-element.10), channel_id=1, source_target_pairs={{0,4},{2,6},{4,8},{6,10},{8,12},{10,14},{1,5},{3,7},{5,9},{7,11},{... | collective-permute-start | bytes 2555912 | tf_op jit(solution)/shard_map/ppermute | solution.py:358
  202.2 26.5 %collective-permute-start.2 = (bf16[256,1664]{1,0:T(8,128)(2,1)}, bf16[256,1664]{1,0:T(8,128)(2,1)}, u32[]{:S(2)}, u32[]{:S(2)}) collective-permute-start(bf16[256,1664]{1,0:T(8,128)(2,1)} %get-tuple-element.11), channel_id=1, source_target_pairs={{4,0},{6,2},{8,4},{10,6},{12,8},{14,10},{5,1},{7,3},{9,5},{11,7},{... | collective-permute-start | bytes 2555912 | tf_op jit(solution)/shard_map/ppermute | solution.py:359
Sparse Core Ops, SparseCore 0:
  17.4 74.2 all-reduce.1

commit v4 on v3

--- a/solution.py
+++ b/solution.py
@@ -253,19 +253,21 @@
                 rows = pl.ds(pl.multiple_of(at * 16, 16), 16)
                 out_ref[term, rows, :] = own[step, rows, :] + recv_x[step, rows, :].astype(jnp.float32)
 
-    for step in range(line):
+    lead = line + 2
+    for step in range(lead):
         produce(step)
         if step == 0:
             gather(0)
-    done = 0
-    for step in range(line, steps):
-        finish(done)
-        done += 1
-        produce(step)
-        if done < line:
-            gather(done)
-    for step in range(done, steps - 1):
+    hop = 1
+    for step in range(steps - 1):
         finish(step)
+        if lead + step < steps:
+            produce(lead + step)
+        if step % 2 and hop < line:
+            gather(hop)
+            hop += 1
+    for rest in range(hop, line):
+        gather(rest)
     for step in range(steps - 1):
         x_copy(step).wait_send()
         if step < line - 1:

time: 240 us -> 226 us (0.942)
  starting transfers between devices: 22.1 us -> 12.1 us
  Pallas kernels: 163 us -> 159 us
    ppermute x1, starting transfers between devices: 18.4 us -> 9.76 us  [per_device(): lax.ppermute(up_hop, 'row', [(at, at + 2) for at in range(rows - 2)])]
    pallas_call x1, Pallas kernels: 163 us -> 159 us  [reduce_terms(): pl.pallas_call(functools.partial(scatter_kernel, line), out_shape=(jax.Sh...]
  transfers between devices with their start and end apart: 4 -> 4, of which waited for: 0 -> 0; matrix products, arithmetic and copies ran while one was open for 11% -> 12% of each run, Pallas kernels for 68% -> 70%
where the time goes in v4:
time: 226 us
  Pallas kernels  159 us (70%)
  matrix products  30.7 us (14%)
  between operations  18 us (8%)
  starting transfers between devices  12.1 us (5%)
  local copies, waits for them, and re-layouts  3.6 us (2%)
    pallas_call x1, Pallas kernels, reduce_terms(): pl.pallas_call(functools.partial(scatter_kernel, line), out_shape=(jax.Sh...  159 us
    dot_general x1, matrix products, merge_panel(): jnp.dot(left_panel, right_panel, preferred_element_type=jnp.float32)  23.2 us
    ppermute x1, starting transfers between devices, per_device(): lax.ppermute(up_hop, 'row', [(at, at + 2) for at in range(rows - 2)])  9.76 us
  transfers between devices with their start and end apart: 4, of which 0 were waited for; matrix products, arithmetic and copies ran while one was open for 12% of the time, Pallas kernels for 70%

profile of v4, /device:TPU:0, one launch (start us, length us, event | category | flops | bytes accessed | tf_op | source)
XLA Modules:
  0.0 226.1 jit_solution(937547954497391106)
XLA Ops:
  7.2 0.0 copy-start.1
  7.2 0.0 all-reduce.2.cloned.1.call-start
  7.2 1.3 fusion.25
  12.4 1.1 dynamic-slice_bitcast_fusion.1
  13.5 0.1 fusion.24
  13.7 0.0 copy-done.1
  13.7 2.3 %all_gather.3.tok_ref = bf16[256,1024]{1,0:T(8,128)(2,1)S(1)} all-gather(bf16[128,1024]{1,0:T(8,128)(2,1)S(1)} %copy-done.1), channel_id=1, replica_groups=mesh['groups'=2,'row'=8,'col'=2] {'col'}, dimensions={0}, use_global_device_ids=true | all-gather | bytes 786432 | tf_op jit(solution)/shard_map/all_gather | solution.py:348
  15.9 0.0 copy-start
  16.0 1.3 convolution_bitcast_fusion
  17.2 0.0 all-reduce.2.cloned.1.call-update
  17.3 1.1 dynamic-slice_bitcast_fusion.3
  18.3 0.8 pad_maximum_fusion.right_ref
  19.1 0.0 copy-done
  19.1 158.6 %shard_map.77 = (f32[2,256,1664]{2,1,0:T(8,128)}, bf16[256,1664]{1,0:T(8,128)(2,1)}, bf16[256,1664]{1,0:T(8,128)(2,1)}, bf16[256,1664]{1,0:T(8,128)(2,1)}, bf16[128,13312]{1,0:T(8,128)(2,1)}) custom-call(bf16[256,1024]{1,0:T(8,128)(2,1)} %copy-done, bf16[1024,13312]{1,0:T(8,128)(2,1)} %up_ref.1, bf16[1024,13312]{1,0:T(8,128)(2,1)} %gate_ref.1, ...), custom_call_target="tpu_custom_call" | custom-call | flops 13958643712 | bytes 54525952 | tf_op jit(solution)/shard_map/pallas_call | solution.py:287
  177.8 0.8 collective-permute-start
  178.6 9.8 %collective-permute-start.1 = (bf16[256,1664]{1,0:T(8,128)(2,1)}, bf16[256,1664]{1,0:T(8,128)(2,1)S(1)}, u32[]{:S(2)}, u32[]{:S(2)}) collective-permute-start(bf16[256,1664]{1,0:T(8,128)(2,1)} %get-tuple-element.10), channel_id=1, source_target_pairs={{0,4},{2,6},{4,8},{6,10},{8,12},{10,14},{1,5},{3,7},{5,9},{7,11},{... | collective-permute-start | bytes 2555912 | tf_op jit(solution)/shard_map/ppermute | solution.py:360
  188.3 1.5 collective-permute-start.2
  189.8 23.2 %add_convert_fusion = bf16[1024,13312]{1,0:T(8,128)(2,1)} fusion(bf16[1024,13312]{1,0:T(8,128)(2,1)} %gate_ref.1, bf16[128,13312]{1,0:T(8,128)(2,1)} %get-tuple-element.7, bf16[1024,64]{1,0:T(8,128)(2,1)S(1)} %slice_negate_fusion, bf16[1024,64]{1,0:T(8,128)(2,1)S(1)} %get-tuple-element.17), kind=kOutput, calls=%fused_computation | convolution fusion | flops 3531079680 | bytes 58195968 | tf_op jit(solution)/shard_map/dot_general | solution.py:12
  213.0 0.0 all-reduce.2.cloned.1.call-done
  213.0 1.8 fusion.14
  214.8 0.0 collective-permute-done
  214.8 0.0 collective-permute-done.1
  214.8 0.0 collective-permute-done.2
  214.8 4.4 %multiply_convert_fusion = bf16[256,1664]{1,0:T(8,128)(2,1)} fusion(f32[256,1664]{1,0:T(8,128)S(1)} %fusion.14, bf16[256,1664]{1,0:T(8,128)(2,1)} %collective-permute-done.2, bf16[256,1664]{1,0:T(8,128)(2,1)S(1)} %collective-permute-done.1, bf16[256,1664]{1,0:T(8,128)(2,1)S(1)} %collective-permute-done, f32[2,256,1664]{2,1,0:T(8,128)} %get-tuple-element.8, ...), kind=kOutput, calls=%fused_computation.7 | convolution fusion | flops 61374464 | bytes 8798212 | tf_op jit(solution)/shard_map/dot_general | solution.py:392
  (1 shorter events, 0.0 us)
Async XLA Ops:
  7.2 6.5 %copy-start.1 = (bf16[128,1024]{1,0:T(8,128)(2,1)S(1)}, bf16[128,1024]{1,0:T(8,128)(2,1)}, u32[]{:S(2)}) copy-start(bf16[128,1024]{1,0:T(8,128)(2,1)} %param.6) | copy-start | bytes 786436
  7.2 205.8 %all-reduce.2.cloned.1.call-start = ((), (), s32[]{:S(2)}) async-start(), calls=%async_computation | async-start | bytes 393216 | tf_op jit(solution)/shard_map/psum | solution.py:354
  15.9 3.2 %copy-start = (bf16[256,1024]{1,0:T(8,128)(2,1)}, bf16[256,1024]{1,0:T(8,128)(2,1)S(1)}, u32[]{:S(2)}) copy-start(bf16[256,1024]{1,0:T(8,128)(2,1)S(1)} %all_gather.3.tok_ref) | copy-start | bytes 1572868
  177.8 37.0 %collective-permute-start = (bf16[256,1664]{1,0:T(8,128)(2,1)}, bf16[256,1664]{1,0:T(8,128)(2,1)S(1)}, u32[]{:S(2)}, u32[]{:S(2)}) collective-permute-start(bf16[256,1664]{1,0:T(8,128)(2,1)} %get-tuple-element.9), channel_id=1, source_target_pairs={{0,2},{2,0},{4,6},{6,4},{8,10},{10,8},{12,14},{14,12},{1,3},{3,1},... | collective-permute-start | bytes 2555912 | tf_op jit(solution)/shard_map/ppermute | solution.py:362
  178.6 36.2 %collective-permute-start.1 = (bf16[256,1664]{1,0:T(8,128)(2,1)}, bf16[256,1664]{1,0:T(8,128)(2,1)S(1)}, u32[]{:S(2)}, u32[]{:S(2)}) collective-permute-start(bf16[256,1664]{1,0:T(8,128)(2,1)} %get-tuple-element.10), channel_id=1, source_target_pairs={{0,4},{2,6},{4,8},{6,10},{8,12},{10,14},{1,5},{3,7},{5,9},{7,11},{... | collective-permute-start | bytes 2555912 | tf_op jit(solution)/shard_map/ppermute | solution.py:360
  188.3 26.5 %collective-permute-start.2 = (bf16[256,1664]{1,0:T(8,128)(2,1)}, bf16[256,1664]{1,0:T(8,128)(2,1)}, u32[]{:S(2)}, u32[]{:S(2)}) collective-permute-start(bf16[256,1664]{1,0:T(8,128)(2,1)} %get-tuple-element.11), channel_id=1, source_target_pairs={{4,0},{6,2},{8,4},{10,6},{12,8},{14,10},{5,1},{7,3},{9,5},{11,7},{... | collective-permute-start | bytes 2555912 | tf_op jit(solution)/shard_map/ppermute | solution.py:361
Sparse Core Ops, SparseCore 0:
  17.4 74.3 all-reduce.1
